TPU v7x, 32 devices: a whole 2x2x4 slice. The times are simulated.
32 devices in a mesh: feat: 4 (over x, core), samp: 8 (over z, y).
Axes of the slice: x: 2, y: 2, z: 4, core: 2. Of those that a mesh axis runs over, the one named last changes fastest.
Arguments:
- tier_one: bfloat16 [8192, 3072], P('feat', 'samp')
- residuals: bfloat16 [3072, 128], P('samp'), may hold values from -6 to 6
- pair_list: int32 [3, 16384], P(None, 'feat'), may hold values from 0 to 8191, as said below
Outputs:
- scores: float32 [16384, 128], P(('feat', 'samp'))
Inputs may be any that keep to these rules, and one draw needn't show every extreme that they name: `pair_list`: rows 0 and 1 are feature indices, row 2 an operator id of 0 to 3; each descriptor's two features differ.
All inputs are finite; a program needn't handle non-finite values.
Results may differ from a plain program's by a relative error of at most 0.0031.
Values may be sent and summed in bfloat16 or wider, within the bound.
A program may use at most 64 MiB of HBM per device.

v0:
```python
import functools
import math

import jax
import jax.numpy as jnp
from jax import lax
from jax.experimental import pallas as pl
from jax.experimental.pallas import tpu as pltpu
from jax.sharding import PartitionSpec as P

epsilon = 1e-05
MESH = pl.DeviceIdType.MESH
lanes = 128


def kernel(
    sizes, tier_ref, res_any, pair_any, out_ref,
    res_ref, pair_smem, pair_vmem, slots, table, first_even, second_even, first_odd, second_odd,
    op_wide, weights, share_block, stats_wide,
    near_out, near_in, line_out, line_in, send_stats, recv_stats, turned, scale,
    own_sem, small_sems, cross_send, cross_recv, sib_send, sib_recv, relay_send, relay_recv,
    near_send, near_recv, line_send, line_recv, stats_send, stats_recv,
):
    n_feat, n_samp, rows, samples, pairs, chunks = sizes
    chips = n_feat // 2
    pieces = samples // lanes
    owned = pairs // n_samp
    sub = min(owned // 2, 128)
    group, tall = 8, 16
    step = rows // chunks
    total_samples = samples * n_samp
    feat = lax.axis_index("feat")
    samp = lax.axis_index("samp")
    chip = feat // 2
    core = lax.rem(feat, 2)
    sibling = chip * 2 + 1 - core
    half = n_samp // 2
    high = samp // 2
    low = lax.rem(samp, 2)
    partner = high * 2 + 1 - low

    def far(offset):
        return lax.rem(chip + offset, chips) * 2 + core

    barrier = pltpu.get_barrier_semaphore()
    pl.semaphore_signal(barrier, inc=1, device_id=(sibling, samp), device_id_type=MESH)
    for offset in range(1, chips):
        pl.semaphore_signal(barrier, inc=1, device_id=(far(offset), samp), device_id_type=MESH)
    for offset in range(1, n_samp):
        pl.semaphore_signal(
            barrier, inc=1, device_id=(feat, lax.rem(samp + offset, n_samp)), device_id_type=MESH
        )
    own_copy = pltpu.make_async_copy(tier_ref, slots.at[feat], own_sem)
    own_copy.start()
    pl.semaphore_wait(barrier, 1 + (chips - 1) + (n_samp - 1))

    def part(index):
        return pl.ds(pl.multiple_of(index * step, step), step)

    def cross(offset, k, holder, target):
        return pltpu.make_async_remote_copy(
            src_ref=tier_ref.at[part(k)],
            dst_ref=slots.at[holder, part(k)],
            send_sem=cross_send.at[offset - 1, k],
            recv_sem=cross_recv.at[offset - 1, k],
            device_id=(target, samp),
            device_id_type=MESH,
        )

    def relay(offset, k, holder):
        return pltpu.make_async_remote_copy(
            src_ref=slots.at[holder, part(k)],
            dst_ref=slots.at[holder, part(k)],
            send_sem=relay_send.at[offset - 1, k],
            recv_sem=relay_recv.at[offset - 1, k],
            device_id=(sibling, samp),
            device_id_type=MESH,
        )

    def to_sibling(holder):
        return pltpu.make_async_remote_copy(
            src_ref=tier_ref,
            dst_ref=slots.at[holder],
            send_sem=sib_send,
            recv_sem=sib_recv,
            device_id=(sibling, samp),
            device_id_type=MESH,
        )

    for offset in range(1, chips):
        @pl.loop(0, chunks)
        def _(k):
            cross(offset, k, feat, far(offset)).start()
    to_sibling(feat).start()

    flat = table.reshape(n_feat * rows * 4, lanes)

    def widen(holder, k):
        @pl.loop(0, step // 64 if step % 64 == 0 else 1)
        def _(g):
            size = 64 if step % 64 == 0 else step
            start = pl.multiple_of(k * step + g * size, size)
            for j in range(pieces):
                values = slots[holder, pl.ds(start, size), j * lanes:(j + 1) * lanes]
                flat[pl.ds(4 * (holder * rows + start) + j, size, stride=4), :] = values.astype(jnp.float32)

    small_copies = [
        pltpu.make_async_copy(pair_any, pair_vmem, small_sems.at[0]),
        pltpu.make_async_copy(res_any, res_ref, small_sems.at[1]),
        pltpu.make_async_copy(pair_any, pair_smem, small_sems.at[2]),
    ]
    for copy in small_copies:
        copy.start()
    for copy in small_copies:
        copy.wait()

    weights[:, :lanes] = res_ref[...]
    weights[:, lanes:] = jnp.ones((samples, lanes), jnp.bfloat16)
    col_local = jnp.sum(res_ref[...].astype(jnp.float32), axis=0, keepdims=True)

    @pl.loop(0, pairs // lanes)
    def _(g):
        span = pl.ds(pl.multiple_of(g * lanes, lanes), lanes)
        op_wide[span, :] = jnp.broadcast_to(pair_vmem[g, 2:3, :], (lanes, lanes)).T

    own_copy.wait()

    @pl.loop(0, chunks)
    def _(k):
        widen(feat, k)

    to_sibling(sibling).wait_recv()

    @pl.loop(0, chunks)
    def _(k):
        widen(sibling, k)

    for offset in range(1, chips):
        mine = far(chips - offset)
        theirs = mine + 1 - 2 * core

        @pl.loop(0, chunks)
        def _(k):
            cross(offset, k, mine, feat).wait_recv()
            relay(offset, k, mine).start()
            widen(mine, k)

            @pl.when(k > 0)
            def _():
                relay(offset, k - 1, theirs).wait_recv()
                widen(theirs, k - 1)

        relay(offset, chunks - 1, theirs).wait_recv()
        widen(theirs, chunks - 1)

    lane_id = lax.broadcasted_iota(jnp.int32, (sub, lanes), 1)

    couples = owned // (2 * sub)
    count = half * couples
    lead = count * 5 // 8

    def unit(r):
        k = r - lead
        mixed = r < 2 * count - lead
        ours = jnp.where(r < lead, 0, jnp.where(mixed, lax.rem(k + 1, 2), 1))
        m = jnp.where(r < lead, r, jnp.where(mixed, k // 2 + lead * lax.rem(k, 2), r - count))
        t = m // couples
        h = lax.rem(m, couples)
        owner = lax.rem(high + 1 + t, half) * 2 + lax.rem(low + 1 + ours, 2)
        return ours, m, t, h, owner

    def base_of(r):
        _, _, _, h, owner = unit(r)
        return owner * owned + h * (2 * sub)

    def index_of(which, base, p):
        inside = 0 if sub % lanes == 0 else lax.rem(base, lanes)
        return pair_smem[base // lanes, which, inside + p]

    def fetch(base, p):
        return (
            [table[index_of(0, base, p + u)] for u in range(group)],
            [table[index_of(1, base, p + u)] for u in range(group)],
        )

    def stage(stages, p, fetched):
        for u in range(group):
            stages[0][4 * (p + u):4 * (p + u) + 4, :] = fetched[0][u]
            stages[1][4 * (p + u):4 * (p + u) + 4, :] = fetched[1][u]

    def build(stages, base, p):
        op = op_wide[pl.ds(pl.multiple_of(base + p, tall), tall), :]
        parts = []
        square = jnp.zeros((tall, lanes), jnp.float32)
        for j in range(pieces):
            a = stages[0][pl.ds(4 * p + j, tall, stride=4), :]
            b = stages[1][pl.ds(4 * p + j, tall, stride=4), :]
            plain = a + jnp.where(op == 1, -b, b)
            other = jnp.where(op == 2, a * b, a / (1.0 + jnp.abs(b)))
            built = jnp.where(op < 2, plain, other).astype(jnp.bfloat16)
            parts.append(built)
            wide = built.astype(jnp.float32)
            square += wide * wide
        return jnp.concatenate(parts, axis=1), jnp.sum(square, axis=1, keepdims=True)

    def advance(now, base, later, next_base, here):
        built, squares = [], []
        steps = sub // tall
        share = sub // 2 // steps
        fetched = fetch(next_base, 0)
        for i in range(steps):
            one, square = build(now, base, i * tall)
            built.append(one)
            squares.append(square)
            for p in range(i * share, (i + 1) * share, group):
                following = fetch(next_base, p + group)
                stage(later, p, fetched)
                fetched = following
        both = jnp.dot(
            jnp.concatenate(built, axis=0), weights[...], preferred_element_type=jnp.float32
        )
        for p in range(sub // 2, sub, group):
            following = fetch(next_base, p + group) if p + group < sub else None
            stage(later, p, fetched)
            fetched = following
        sums = both[:, lanes:]
        share_block[here, :] = both[:, :lanes] - sums * (col_local / samples)
        stats_wide[here, :] = jnp.where(lane_id == 0, sums, jnp.concatenate(squares, axis=0))

    even = (first_even, second_even)
    odd = (first_odd, second_odd)

    @pl.loop(0, sub // group)
    def _(g):
        base = base_of(0)
        firsts = [table[index_of(0, base, g * group + u)] for u in range(group)]
        seconds = [table[index_of(1, base, g * group + u)] for u in range(group)]
        for u in range(group):
            spot = pl.ds(pl.multiple_of((g * group + u) * 4, 4), 4)
            first_even[spot, :] = firsts[u]
            second_even[spot, :] = seconds[u]

    def rows_of(h):
        return pl.ds(pl.multiple_of(h * (2 * sub), 2 * sub), 2 * sub)

    def near_copy(m):
        t, here = m // couples, rows_of(lax.rem(m, couples))
        return pltpu.make_async_remote_copy(
            src_ref=near_out.at[t, here],
            dst_ref=near_in.at[t, here],
            send_sem=near_send.at[m],
            recv_sem=near_recv.at[m],
            device_id=(feat, partner),
            device_id_type=MESH,
        )

    def line_copy(m, source, target):
        t, h = m // couples, lax.rem(m, couples)
        return pltpu.make_async_remote_copy(
            src_ref=line_out.at[t, rows_of(h)],
            dst_ref=line_in.at[source, rows_of(h)],
            send_sem=line_send.at[m],
            recv_sem=line_recv.at[source * couples + h],
            device_id=(feat, target * 2 + low),
            device_id_type=MESH,
        )

    def stats_copy(owner, source):
        return pltpu.make_async_remote_copy(
            src_ref=send_stats.at[owner],
            dst_ref=recv_stats.at[source],
            send_sem=stats_send.at[owner],
            recv_sem=stats_recv.at[source],
            device_id=(feat, owner),
            device_id_type=MESH,
        )

    @pl.loop(0, 2 * count)
    def _(r):
        ours, m, t, h, owner = unit(r)
        base = owner * owned + h * (2 * sub)
        advance(even, base, odd, base + sub, pl.ds(0, sub))
        advance(odd, base + sub, even, base_of(r + 1), pl.ds(sub, sub))
        for q in range(2 * sub // lanes):
            flipped = stats_wide[q * lanes:(q + 1) * lanes, :].T
            span = pl.ds(pl.multiple_of(h * (2 * sub) + q * lanes, lanes), lanes)
            send_stats[owner, 0:2, span] = flipped[0:2, :]
        send_stats[owner, 2:3, 0:lanes] = col_local
        here = rows_of(h)

        @pl.when(ours == 0)
        def _():
            near_out[t, here, :] = share_block[...].astype(jnp.bfloat16)
            near_copy(m).start()

        @pl.when(ours == 1)
        def _():
            near_copy(m).wait_recv()
            total = share_block[...] + near_in[t, here, :].astype(jnp.float32)
            line_out[t, here, :] = total.astype(jnp.bfloat16)
            out_ref[here, :] = total

            @pl.when(t < half - 1)
            def _():
                line_copy(m, high, lax.rem(high + 1 + t, half)).start()

        @pl.when((h == couples - 1) & (r < 2 * count - 1))
        def _():
            stats_copy(owner, samp).start()

    recv_stats[samp] = send_stats[samp]

    @pl.loop(1, n_samp)
    def _(t):
        stats_copy(samp, lax.rem(samp + n_samp - t, n_samp)).wait_recv()

    first_sums = jnp.zeros((1, owned), jnp.float32)
    square_sums = jnp.zeros((1, owned), jnp.float32)
    for d in range(n_samp):
        first_sums += recv_stats[d, 0:1, :]
        square_sums += recv_stats[d, 1:2, :]
    means = first_sums / total_samples
    variance = square_sums / total_samples - means * means
    turned[n_samp:n_samp + 1, :] = lax.rsqrt(variance + epsilon) / math.sqrt(total_samples)
    for d in range(n_samp):
        turned[d:d + 1, :] = recv_stats[d, 0:1, :] / samples - means

    @pl.loop(0, owned // lanes)
    def _(q):
        span = pl.ds(pl.multiple_of(q * lanes, lanes), lanes)
        columns = turned[:, span].T
        total = out_ref[span, :]
        for d in range(n_samp):
            total += columns[:, d:d + 1] * recv_stats[d, 2:3, 0:lanes]
        out_ref[span, :] = total
        scale[span, :] = jnp.broadcast_to(columns[:, n_samp:n_samp + 1], (lanes, lanes))

    @pl.loop(0, (half - 1) * couples)
    def _(m):
        source = lax.rem(high + half - 1 - m // couples, half)
        here = rows_of(lax.rem(m, couples))
        line_copy(m, source, high).wait_recv()
        out_ref[here, :] += line_in[source, here, :].astype(jnp.float32)

    out_ref[...] *= scale[...]

    to_sibling(feat).wait_send()
    for offset in range(1, chips):
        @pl.loop(0, chunks)
        def _(k):
            cross(offset, k, feat, far(offset)).wait_send()
            relay(offset, k, far(chips - offset)).wait_send()

    @pl.loop(0, count)
    def _(m):
        near_copy(m).wait_send()

    @pl.loop(0, (half - 1) * couples)
    def _(m):
        line_copy(m, high, lax.rem(high + 1 + m // couples, half)).wait_send()

    @pl.loop(1, n_samp)
    def _(t):
        stats_copy(lax.rem(samp + t, n_samp), samp).wait_send()


def per_device(n_feat, n_samp, tier_one, residuals, pair_list):
    rows, samples = tier_one.shape
    pairs = pair_list.shape[1]
    chips = n_feat // 2
    owned = pairs // n_samp
    sub = min(owned // 2, 128)
    chunks = 16
    sizes = (n_feat, n_samp, rows, samples, pairs, chunks)
    dma = pltpu.SemaphoreType.DMA
    tiled = pair_list.reshape(3, pairs // lanes, lanes).transpose(1, 0, 2)
    return pl.pallas_call(
        functools.partial(kernel, sizes),
        out_shape=jax.ShapeDtypeStruct((owned, lanes), jnp.float32),
        in_specs=[
            pl.BlockSpec(memory_space=pl.ANY),
            pl.BlockSpec(memory_space=pl.ANY),
            pl.BlockSpec(memory_space=pl.ANY),
        ],
        out_specs=pl.BlockSpec(memory_space=pltpu.VMEM),
        scratch_shapes=[
            pltpu.VMEM((samples, lanes), jnp.bfloat16),
            pltpu.SMEM((pairs // lanes, 3, lanes), jnp.int32),
            pltpu.VMEM((pairs // lanes, 3, lanes), jnp.int32),
            pltpu.VMEM((n_feat, rows, samples), jnp.bfloat16),
            pltpu.VMEM((n_feat * rows, 4, lanes), jnp.float32),
            pltpu.VMEM((sub * 4, lanes), jnp.float32),
            pltpu.VMEM((sub * 4, lanes), jnp.float32),
            pltpu.VMEM((sub * 4, lanes), jnp.float32),
            pltpu.VMEM((sub * 4, lanes), jnp.float32),
            pltpu.VMEM((pairs, lanes), jnp.int32),
            pltpu.VMEM((samples, 2 * lanes), jnp.bfloat16),
            pltpu.VMEM((2 * sub, lanes), jnp.float32),
            pltpu.VMEM((2 * sub, lanes), jnp.float32),
            pltpu.VMEM((n_samp // 2, owned, lanes), jnp.bfloat16),
            pltpu.VMEM((n_samp // 2, owned, lanes), jnp.bfloat16),
            pltpu.VMEM((n_samp // 2, owned, lanes), jnp.bfloat16),
            pltpu.VMEM((n_samp // 2, owned, lanes), jnp.bfloat16),
            pltpu.VMEM((n_samp, 4, owned), jnp.float32),
            pltpu.VMEM((n_samp, 4, owned), jnp.float32),
            pltpu.VMEM((lanes, owned), jnp.float32),
            pltpu.VMEM((owned, lanes), jnp.float32),
            dma,
            dma((3,)),
            dma((max(chips - 1, 1), chunks)),
            dma((max(chips - 1, 1), chunks)),
            dma,
            dma,
            dma((max(chips - 1, 1), chunks)),
            dma((max(chips - 1, 1), chunks)),
            dma((n_samp // 2 * (owned // (2 * sub)),)),
            dma((n_samp // 2 * (owned // (2 * sub)),)),
            dma((n_samp // 2 * (owned // (2 * sub)),)),
            dma((n_samp // 2 * (owned // (2 * sub)),)),
            dma((n_samp,)),
            dma((n_samp,)),
        ],
        compiler_params=pltpu.CompilerParams(
            collective_id=0, has_side_effects=True, vmem_limit_bytes=56 * 2**20
        ),
    )(tier_one, residuals, tiled)


def solution(mesh):
    in_specs = (P("feat", "samp"), P("samp", None), P(None, "feat"))
    out_specs = P(("feat", "samp"), None)
    return jax.shard_map(
        functools.partial(per_device, mesh.shape["feat"], mesh.shape["samp"]),
        mesh=mesh, in_specs=in_specs, out_specs=out_specs, check_vma=False,
    )
```

profile of v0, /device:TPU:0, one launch (start us, length us, event | category | flops | bytes accessed | tf_op | source)
XLA Modules:
  0.0 66.6 jit_solution(8941456129466596208)
XLA Ops:
  0.0 65.0 %shard_map.37 = f32[512,128]{1,0:T(8,128)} custom-call(bf16[2048,384]{1,0:T(8,128)(2,1)} %tier_ref.1, bf16[384,128]{1,0:T(8,128)(2,1)} %res_any.1, s32[32,3,128]{2,1,0:T(4,128)} %bitcast.3), custom_call_target="tpu_custom_call" | custom-call | tf_op jit(solution)/shard_map/pallas_call | solution.py:377
  65.0 1.7 %copy.5 = f32[512,128]{1,0:T(8,128)} copy(f32[512,128]{1,0:T(8,128)} %shard_map.37) | data formatting | bytes 524288
where the time goes:
time: 66.9 us; the launch traced here: 66.6 us
  Pallas kernels  65 us (97%)
  local copies, waits for them, and re-layouts  1.67 us (2%)
    pallas_call x1, Pallas kernels, per_device(): pl.pallas_call(functools.partial(kernel, sizes), out_shape=jax.ShapeDtype...  65 us
    unnamed x1, local copies, waits for them, and re-layouts  1.67 us

commit v1 on v0

--- a/solution.py
+++ b/solution.py
@@ -185,16 +185,16 @@
 
     def stage(stages, p, fetched):
         for u in range(group):
-            stages[0][4 * (p + u):4 * (p + u) + 4, :] = fetched[0][u]
-            stages[1][4 * (p + u):4 * (p + u) + 4, :] = fetched[1][u]
+            stages[0][pieces * (p + u):pieces * (p + u + 1), :] = fetched[0][u][:pieces]
+            stages[1][pieces * (p + u):pieces * (p + u + 1), :] = fetched[1][u][:pieces]
 
     def build(stages, base, p):
         op = op_wide[pl.ds(pl.multiple_of(base + p, tall), tall), :]
         parts = []
         square = jnp.zeros((tall, lanes), jnp.float32)
         for j in range(pieces):
-            a = stages[0][pl.ds(4 * p + j, tall, stride=4), :]
-            b = stages[1][pl.ds(4 * p + j, tall, stride=4), :]
+            a = stages[0][pl.ds(pieces * p + j, tall, stride=pieces), :]
+            b = stages[1][pl.ds(pieces * p + j, tall, stride=pieces), :]
             plain = a + jnp.where(op == 1, -b, b)
             other = jnp.where(op == 2, a * b, a / (1.0 + jnp.abs(b)))
             built = jnp.where(op < 2, plain, other).astype(jnp.bfloat16)
@@ -236,9 +236,9 @@
         firsts = [table[index_of(0, base, g * group + u)] for u in range(group)]
         seconds = [table[index_of(1, base, g * group + u)] for u in range(group)]
         for u in range(group):
-            spot = pl.ds(pl.multiple_of((g * group + u) * 4, 4), 4)
-            first_even[spot, :] = firsts[u]
-            second_even[spot, :] = seconds[u]
+            spot = pl.ds(pl.multiple_of(g * (group * pieces), 8) + pieces * u, pieces)
+            first_even[spot, :] = firsts[u][:pieces]
+            second_even[spot, :] = seconds[u][:pieces]
 
     def rows_of(h):
         return pl.ds(pl.multiple_of(h * (2 * sub), 2 * sub), 2 * sub)
@@ -389,10 +389,10 @@
             pltpu.VMEM((pairs // lanes, 3, lanes), jnp.int32),
             pltpu.VMEM((n_feat, rows, samples), jnp.bfloat16),
             pltpu.VMEM((n_feat * rows, 4, lanes), jnp.float32),
-            pltpu.VMEM((sub * 4, lanes), jnp.float32),
-            pltpu.VMEM((sub * 4, lanes), jnp.float32),
-            pltpu.VMEM((sub * 4, lanes), jnp.float32),
-            pltpu.VMEM((sub * 4, lanes), jnp.float32),
+            pltpu.VMEM((sub * (samples // lanes), lanes), jnp.float32),
+            pltpu.VMEM((sub * (samples // lanes), lanes), jnp.float32),
+            pltpu.VMEM((sub * (samples // lanes), lanes), jnp.float32),
+            pltpu.VMEM((sub * (samples // lanes), lanes), jnp.float32),
             pltpu.VMEM((pairs, lanes), jnp.int32),
             pltpu.VMEM((samples, 2 * lanes), jnp.bfloat16),
             pltpu.VMEM((2 * sub, lanes), jnp.float32),

time: 66.9 us -> 66.9 us (level)
  no operation moved by 1% of the time
where the time goes in v1:
time: 66.9 us; the launch traced here: 66.7 us
  Pallas kernels  65 us (97%)
  local copies, waits for them, and re-layouts  1.67 us (2%)
    pallas_call x1, Pallas kernels, per_device(): pl.pallas_call(functools.partial(kernel, sizes), out_shape=jax.ShapeDtype...  65 us
    unnamed x1, local copies, waits for them, and re-layouts  1.67 us

profile of v1, /device:TPU:0, one launch (start us, length us, event | category | flops | bytes accessed | tf_op | source)
XLA Modules:
  0.0 66.7 jit_solution(4873746138593745434)
XLA Ops:
  0.0 65.0 %shard_map.37 = f32[512,128]{1,0:T(8,128)} custom-call(bf16[2048,384]{1,0:T(8,128)(2,1)} %tier_ref.1, bf16[384,128]{1,0:T(8,128)(2,1)} %res_any.1, s32[32,3,128]{2,1,0:T(4,128)} %bitcast.3), custom_call_target="tpu_custom_call" | custom-call | tf_op jit(solution)/shard_map/pallas_call | solution.py:377
  65.0 1.7 %copy.5 = f32[512,128]{1,0:T(8,128)} copy(f32[512,128]{1,0:T(8,128)} %shard_map.37) | data formatting | bytes 524288

commit v2 on v0

--- a/solution.py
+++ b/solution.py
@@ -157,7 +157,7 @@
 
     couples = owned // (2 * sub)
     count = half * couples
-    lead = count * 5 // 8
+    lead = count * 3 // 8
 
     def unit(r):
         k = r - lead

time: 66.9 us -> 66.2 us (0.990)
  Pallas kernels: 65 us -> 64.3 us
where the time goes in v2:
time: 66.2 us; the launch traced here: 66 us
  Pallas kernels  64.3 us (97%)
  local copies, waits for them, and re-layouts  1.67 us (3%)
    pallas_call x1, Pallas kernels, per_device(): pl.pallas_call(functools.partial(kernel, sizes), out_shape=jax.ShapeDtype...  64.3 us
    unnamed x1, local copies, waits for them, and re-layouts  1.67 us

profile of v2, /device:TPU:0, one launch (start us, length us, event | category | flops | bytes accessed | tf_op | source)
XLA Modules:
  0.0 66.0 jit_solution(17449324788355838691)
XLA Ops:
  0.0 64.3 %shard_map.37 = f32[512,128]{1,0:T(8,128)} custom-call(bf16[2048,384]{1,0:T(8,128)(2,1)} %tier_ref.1, bf16[384,128]{1,0:T(8,128)(2,1)} %res_any.1, s32[32,3,128]{2,1,0:T(4,128)} %bitcast.3), custom_call_target="tpu_custom_call" | custom-call | tf_op jit(solution)/shard_map/pallas_call | solution.py:377
  64.3 1.7 %copy.5 = f32[512,128]{1,0:T(8,128)} copy(f32[512,128]{1,0:T(8,128)} %shard_map.37) | data formatting | bytes 524288
